TPU v7x, 512 devices: a whole 4x8x8 slice. The times are simulated.
512 devices in a mesh: ctx: 32 (over y, x), tp: 16 (over z, core).
Axes of the slice: x: 4, y: 8, z: 8, core: 2. Of those that a mesh axis runs over, the one named last changes fastest.
Arguments:
- query_lin: bfloat16 [64, 8192, 128], P('tp', 'ctx'), may hold values from -6 to 6
- key_lin: bfloat16 [64, 8192, 128], P('tp', 'ctx'), may hold values from -6 to 6
- value_lin: bfloat16 [64, 8192, 128], P('tp', 'ctx'), may hold values from -16 to 16
- decay_log: float32 [64, 8192], P('tp', 'ctx'), may hold values from -1 to 0
- norm_gain: float32 [64, 128], P('tp'), may hold values from 0.1 to 1.9
- query_soft: bfloat16 [64, 8192, 128], P('tp', 'ctx'), may hold values from -5 to 5
- key_soft: bfloat16 [64, 8192, 128], P('tp', 'ctx'), may hold values from -5 to 5
- value_soft: bfloat16 [64, 8192, 128], P('tp', 'ctx'), may hold values from -6 to 6
- doc_lengths: int32 [32], replicated, may hold values from 1 to 1024, 8192 in all
Outputs:
- lightning: bfloat16 [64, 8192, 128], P('tp', 'ctx')
- attended: bfloat16 [64, 8192, 128], P('tp', 'ctx')
Inputs may be any that keep to these rules, and one draw needn't show every extreme that they name: `doc_lengths`: each document has at least one token; one has exactly 1024.
All inputs are finite; a program needn't handle non-finite values.
Results may differ from a plain program's by a relative error of at most 0.023.
Values may be sent and summed in bfloat16 or wider, within the bound.
A program may use at most 64 MiB of HBM per device.

v0:
```python
import jax
import jax.numpy as jnp
from jax import lax
from jax.sharding import PartitionSpec as P

SPAN = 4


norm_eps = 1e-06


def entering(part, axis, combine, identity):
    place = lax.axis_index(axis)
    gathered = jax.tree.map(lambda a: lax.all_gather(a, axis), part)
    state = jax.tree.map(lambda a, e: jnp.zeros_like(a) + jnp.asarray(e, a.dtype), part, identity)

    def one(turn, state):
        return combine(
            state, jax.tree.map(lambda a: lax.dynamic_index_in_dim(a, turn, 0, False), gathered)
        )

    return lax.fori_loop(0, place, one, state)


def from_behind(value, axis, steps):
    count = lax.axis_size(axis)
    initial, last = (max(0, -steps), min(count, count - steps))
    return lax.ppermute(value, axis, [(source, source + steps) for source in range(initial, last)])


def document_of(doc_lengths, token_locations):
    doc_ends = jnp.cumsum(doc_lengths)
    return jnp.sum((token_locations[:, None] >= doc_ends[None, :]).astype(jnp.int32), axis=1)


def join_states(earlier, later):
    return (earlier[0] + later[0], jnp.exp(later[0])[:, None, None] * earlier[1] + later[1])


def linear_local(queries, key_rows, values, decays):
    size = decays.shape[1]
    cumulative = jnp.cumsum(decays, axis=1)
    differences = cumulative[:, :, None] - cumulative[:, None, :]
    indices = jnp.arange(size, dtype=jnp.int32)
    causal = indices[:, None] >= indices[None, :]
    factor = jnp.where(causal[None], jnp.exp(jnp.minimum(differences, 0.0)), 0.0)
    scores = jnp.einsum("hte,hse->hts", queries, key_rows, preferred_element_type=jnp.float32)
    weights = (scores * factor).astype(jnp.bfloat16)
    within = jnp.einsum("hts,hse->hte", weights, values, preferred_element_type=jnp.float32)
    scaled = (queries.astype(jnp.float32) * jnp.exp(cumulative)[:, :, None]).astype(jnp.bfloat16)
    block_decay = cumulative[:, -1]
    decayed = (
        key_rows.astype(jnp.float32) * jnp.exp(block_decay[:, None] - cumulative)[:, :, None]
    ).astype(jnp.bfloat16)
    update = jnp.einsum("hse,hsf->hef", decayed, values, preferred_element_type=jnp.float32)
    return (within, scaled, block_decay, update)


def finish_softmax(scores, allowed, scale):
    scores = jnp.where(allowed, scores * scale, -jnp.inf)
    row_max = jnp.max(scores, axis=1, keepdims=True)
    weights = jnp.exp(scores - row_max)
    row_total = jnp.sum(weights, axis=1, keepdims=True)
    return (weights.astype(jnp.bfloat16), row_total)


def dense_head(queries, key_rows, values, allowed, scale):
    scores = jnp.einsum("te,se->ts", queries, key_rows, preferred_element_type=jnp.float32)
    low_weights, row_total = finish_softmax(scores, allowed, scale)
    mixed = jnp.dot(low_weights, values, preferred_element_type=jnp.float32)
    return (mixed / row_total).astype(jnp.bfloat16)


def local(
    query_lin,
    key_lin,
    value_lin,
    decay_log,
    norm_gain,
    query_soft,
    key_soft,
    value_soft,
    doc_lengths,
):
    head_count, row_count, head_width = query_lin.shape
    device_place = lax.axis_index("ctx")
    query_act = jax.nn.silu(query_lin.astype(jnp.float32)).astype(jnp.bfloat16)
    key_act = jax.nn.silu(key_lin.astype(jnp.float32)).astype(jnp.bfloat16)
    within, scaled, block_decay, update = linear_local(query_act, key_act, value_lin, decay_log)
    prefix = entering(
        (block_decay, update),
        "ctx",
        join_states,
        (jnp.zeros_like(block_decay), jnp.zeros_like(update)),
    )
    carried = prefix[1]
    carried_term = jnp.einsum(
        "hte,hef->htf", scaled, carried.astype(jnp.bfloat16), preferred_element_type=jnp.float32
    )
    linear_out = within + carried_term
    squares = jnp.sum(linear_out * linear_out, axis=(0, 2))
    square_total = lax.psum(squares, "tp")
    mean_square = square_total / (head_count * lax.axis_size("tp") * head_width)
    lightning = (
        linear_out * lax.rsqrt(mean_square + norm_eps)[None, :, None] * norm_gain[:, None, :]
    ).astype(jnp.bfloat16)
    mixed_query = (query_soft.astype(jnp.float32) + lightning.astype(jnp.float32)).astype(
        jnp.bfloat16
    )
    stacked = jnp.stack([key_soft, value_soft])
    earlier = []
    moving = stacked
    for distance in range(SPAN):
        moving = from_behind(moving, "ctx", 1)
        earlier.append(moving)
    ordered = earlier[::-1] + [stacked]
    key_values = jnp.concatenate(ordered, axis=2)
    block_count = SPAN + 1
    window = block_count * row_count
    query_pos = device_place * row_count + jnp.arange(row_count, dtype=jnp.int32)
    key_pos = (device_place - SPAN) * row_count + jnp.arange(window, dtype=jnp.int32)
    query_doc = document_of(doc_lengths, query_pos)
    key_doc = document_of(doc_lengths, key_pos)
    allowed = (
        (key_pos[None, :] <= query_pos[:, None])
        & (key_pos[None, :] >= 0)
        & (key_doc[None, :] == query_doc[:, None])
    )
    scale = head_width ** (-0.5)
    attended = lax.map(
        lambda operands: dense_head(operands[0], operands[1], operands[2], allowed, scale),
        (mixed_query, key_values[0], key_values[1]),
    )
    return (lightning, attended)


def solution(mesh):
    in_specs = (
        P("tp", "ctx", None),
        P("tp", "ctx", None),
        P("tp", "ctx", None),
        P("tp", "ctx"),
        P("tp", None),
        P("tp", "ctx", None),
        P("tp", "ctx", None),
        P("tp", "ctx", None),
        P(),
    )
    out_specs = (P("tp", "ctx", None), P("tp", "ctx", None))
    return jax.shard_map(local, mesh=mesh, in_specs=in_specs, out_specs=out_specs, check_vma=False)
```

profile of v0, /device:TPU:63, one launch (start us, length us, event | category | flops | bytes accessed | tf_op | source)
XLA Modules:
  0.0 228.5 jit_solution(9307121945331833172)
XLA Ops:
  7.2 0.7 reshape.133
  8.0 1.2 reduce-window.18
  9.8 2.2 fusion.38
  12.1 1.3 collective-permute-start
  13.4 13.4 %collective-permute-done = bf16[2,4,256,128]{3,2,1,0:T(8,128)(2,1)S(1)} collective-permute-done((bf16[2,4,256,128]{3,2,1,0:T(8,128)(2,1)S(1)}, bf16[2,4,256,128]{3,2,1,0:T(8,128)(2,1)S(1)}, u32[]{:S(2)}, u32[]{:S(2)}) %collective-permute-start) | collective-permute-done | bytes 524320 | tf_op jit(solution)/shard_map/ppermute | solution.py:28
  26.8 1.3 collective-permute-start.1
  28.1 16.1 %collective-permute-done.1 = bf16[2,4,256,128]{3,2,1,0:T(8,128)(2,1)S(1)} collective-permute-done((bf16[2,4,256,128]{3,2,1,0:T(8,128)(2,1)S(1)}, bf16[2,4,256,128]{3,2,1,0:T(8,128)(2,1)S(1)}, u32[]{:S(2)}, u32[]{:S(2)}) %collective-permute-start.1) | collective-permute-done | bytes 524320 | tf_op jit(solution)/shard_map/ppermute | solution.py:28
  44.2 1.3 collective-permute-start.2
  45.5 1.2 dynamic-slice
  47.5 64.5 %all-reduce = f32[128]{0:T(128)S(1)} all-reduce(f32[128]{0:T(128)S(1)} %bitcast_dynamic-update-slice_fusion), channel_id=2, replica_groups=mesh['ctx'=32,'tp'=16] {'ctx'}, use_global_device_ids=true, to_apply=%add | all-reduce | flops 128 | bytes 1024
  112.1 0.1 copy.47
  112.5 1.3 collective-permute-start.3
  114.1 8.8 %collective-permute-done.3 = bf16[2,4,256,128]{3,2,1,0:T(8,128)(2,1)S(1)} collective-permute-done((bf16[2,4,256,128]{3,2,1,0:T(8,128)(2,1)S(1)}, bf16[2,4,256,128]{3,2,1,0:T(8,128)(2,1)S(1)}, u32[]{:S(2)}, u32[]{:S(2)}) %collective-permute-start.3) | collective-permute-done | bytes 524320 | tf_op jit(solution)/shard_map/ppermute | solution.py:28
  123.2 0.2 slice_bitcast_fusion
  123.4 34.5 %while.23 = (s32[]{:T(128)}, f32[4,128,128]{2,1,0:T(8,128)S(1)}, s32[]{:T(128)}, f32[32,4]{1,0:T(8,128)S(1)}, f32[32,4,128,128]{3,2,1,0:T(8,128)}, /*index=5*/s32[]{:T(128)}, s32[]{:T(128)}, s32[]{:T(128)}) while((s32[]{:T(128)}, f32[4,128,128]{2,1,0:T(8,128)S(1)}, s32[]{:T(128)}, f32[32,4]{1,0:T(8,128)S(1)}, f32[32,4,128,128]{3,2,1,0:T(8,128)}, ...), condition=%wide.region_3.4_spmd, body=%wide.region_2.3_spmd.sunk | while | flops 131077 | bytes 786607 | solution.py:22
  123.5 1.1 bitcast_add_fusion.2
  124.6 1.1 bitcast_add_fusion.2
  125.7 1.1 bitcast_add_fusion.2
  126.8 1.1 bitcast_add_fusion.2
  127.9 1.1 bitcast_add_fusion.2
  129.0 1.1 bitcast_add_fusion.2
  130.1 1.1 bitcast_add_fusion.2
  131.3 1.1 bitcast_add_fusion.2
  132.4 1.1 bitcast_add_fusion.2
  133.5 1.1 bitcast_add_fusion.2
  134.6 1.1 bitcast_add_fusion.2
  135.7 1.1 bitcast_add_fusion.2
  136.8 1.1 bitcast_add_fusion.2
  137.9 1.1 bitcast_add_fusion.2
  139.0 1.1 bitcast_add_fusion.2
  140.2 1.1 bitcast_add_fusion.2
  141.3 1.1 bitcast_add_fusion.2
  142.4 1.1 bitcast_add_fusion.2
  143.5 1.1 bitcast_add_fusion.2
  144.6 1.1 bitcast_add_fusion.2
  145.7 1.1 bitcast_add_fusion.2
  146.8 1.1 bitcast_add_fusion.2
  147.9 1.1 bitcast_add_fusion.2
  149.0 1.1 bitcast_add_fusion.2
  150.2 1.1 bitcast_add_fusion.2
  151.3 1.1 bitcast_add_fusion.2
  152.4 1.1 bitcast_add_fusion.2
  153.5 1.1 bitcast_add_fusion.2
  154.6 1.1 bitcast_add_fusion.2
  155.7 1.1 bitcast_add_fusion.2
  156.8 1.1 bitcast_add_fusion.2
  157.9 2.2 fusion.37
  160.1 2.7 %multiply_reduce_fusion = (f32[256]{0:T(256)S(1)}, f32[4,256,128]{1,2,0:T(8,128)}) fusion(f32[4,256,128]{1,2,0:T(8,128)} %fusion.37, bf16[4,256,128]{2,1,0:T(8,128)(2,1)S(1)} %copy-done, f32[4,256]{1,0:T(4,128)S(1)} %bitcast.63, pred[256,256]{1,0:T(8,128)(4,1)S(1)} %iota_compare_fusion, bf16[4,256,128]{2,1,0:T(8,128)(2,1)} %param.13, ...), kind=kOutput, calls=%fused_computation.46 | convolution fusion | flops 137494272 | bytes 1905664 | tf_op jit(solution)/shard_map/hts,hse->hte/dot_general | solution.py:49
  162.8 44.4 %psum.7 = f32[256]{0:T(256)S(1)} all-reduce(f32[256]{0:T(256)S(1)} %get-tuple-element.193), channel_id=1, replica_groups=mesh['ctx'=32,'tp'=16] {'tp'}, use_global_device_ids=true, to_apply=%region_5.6 | all-reduce | flops 256 | bytes 2048 | tf_op jit(solution)/shard_map/psum | solution.py:102
  207.2 1.9 add_convert_fusion
  209.2 11.7 %while.24 = (s32[]{:T(128)}, bf16[4,256,128]{2,1,0:T(8,128)(2,1)}, bf16[4,256,128]{1,2,0:T(8,128)(2,1)}, bf16[4,1280,128]{2,1,0:T(8,128)(2,1)S(1)}, bf16[4,1280,...) while((s32[]{:T(128)}, bf16[4,256,128]{2,1,0:T(8,128)(2,1)}, ...), condition=%wide.region_12.13_spmd.clone, body=%wide.region_9.12_spmd.clone.sunk | while | flops 171441664 | bytes 4746349 | solution.py:130
  209.2 1.5 fusion.64
  210.7 0.4 fusion.65
  211.0 1.0 fusion.66
  212.1 1.5 fusion.64
  213.6 0.4 fusion.65
  214.0 1.0 fusion.66
  215.0 1.5 fusion.64
  216.5 0.4 fusion.65
  216.9 1.0 fusion.66
  217.9 1.5 fusion.64
  219.4 0.4 fusion.65
  219.8 1.0 fusion.66
  220.8 0.8 copy.50
  (78 shorter events, 2.3 us)
Async XLA Ops:
  7.2 2.6 %copy-start = (bf16[4,256,128]{2,1,0:T(8,128)(2,1)S(1)}, bf16[4,256,128]{2,1,0:T(8,128)(2,1)}, u32[]{:S(2)}) copy-start(bf16[4,256,128]{2,1,0:T(8,128)(2,1)} %param.15) | copy-start | bytes 786436
  7.2 116.2 %all-gather.4.cloned.1.call-start = ((), (), s32[]{:S(2)}) async-start(), calls=%async_computation | async-start | bytes 8650752 | tf_op jit(solution)/shard_map/all_gather | solution.py:14
  9.8 2.3 copy-start.1
  9.8 2.3 copy-start.2
  12.0 100.0 %copy-start.3 = (bf16[4,256,128]{2,1,0:T(8,128)(2,1)S(1)}, bf16[4,256,128]{2,1,0:T(8,128)(2,1)}, u32[]{:S(2)}) copy-start(bf16[4,256,128]{2,1,0:T(8,128)(2,1)} %param.18) | copy-start | bytes 786436
  12.0 100.2 %copy-start.5 = (s32[32]{0:T(128)S(1)}, s32[32]{0:T(128)}, u32[]{:S(2)}) copy-start(s32[32]{0:T(128)} %param.21) | copy-start | bytes 388
  12.1 14.7 %collective-permute-start = (bf16[2,4,256,128]{3,2,1,0:T(8,128)(2,1)S(1)}, bf16[2,4,256,128]{3,2,1,0:T(8,128)(2,1)S(1)}, u32[]{:S(2)}, u32[]{:S(2)}) collective-permute-start(bf16[2,4,256,128]{3,2,1,0:T(8,128)(2,1)S(1)} %pad_maximum_fusion), channel_id=1, source_target_pairs={{0,16},{16,32},{32,48},{48,64},{64,80},{80,96},{96,112},{112,128},... | collective-permute-start | bytes 1572872 | tf_op jit(solution)/shard_map/ppermute | solution.py:28
  26.8 17.4 %collective-permute-start.1 = (bf16[2,4,256,128]{3,2,1,0:T(8,128)(2,1)S(1)}, bf16[2,4,256,128]{3,2,1,0:T(8,128)(2,1)S(1)}, u32[]{:S(2)}, u32[]{:S(2)}) collective-permute-start(bf16[2,4,256,128]{3,2,1,0:T(8,128)(2,1)S(1)} %collective-permute-done), channel_id=1, source_target_pairs={{0,16},{16,32},{32,48},{48,64},{64,80},{80,96},{96,112},{112,128},... | collective-permute-start | bytes 1572872 | tf_op jit(solution)/shard_map/ppermute | solution.py:28
  44.2 68.3 %collective-permute-start.2 = (bf16[2,4,256,128]{3,2,1,0:T(8,128)(2,1)S(1)}, bf16[2,4,256,128]{3,2,1,0:T(8,128)(2,1)S(1)}, u32[]{:S(2)}, u32[]{:S(2)}) collective-permute-start(bf16[2,4,256,128]{3,2,1,0:T(8,128)(2,1)S(1)} %collective-permute-done.1), channel_id=1, source_target_pairs={{0,16},{16,32},{32,48},{48,64},{64,80},{80,96},{96,112},{112,128},... | collective-permute-start | bytes 1572872 | tf_op jit(solution)/shard_map/ppermute | solution.py:28
  112.5 10.3 %collective-permute-start.3 = (bf16[2,4,256,128]{3,2,1,0:T(8,128)(2,1)S(1)}, bf16[2,4,256,128]{3,2,1,0:T(8,128)(2,1)S(1)}, u32[]{:S(2)}, u32[]{:S(2)}) collective-permute-start(bf16[2,4,256,128]{3,2,1,0:T(8,128)(2,1)S(1)} %collective-permute-done.2), channel_id=1, source_target_pairs={{0,16},{16,32},{32,48},{48,64},{64,80},{80,96},{96,112},{112,128},... | collective-permute-start | bytes 1572872 | tf_op jit(solution)/shard_map/ppermute | solution.py:28
  160.1 47.2 %copy-start.4 = (f32[4,128]{1,0:T(4,128)S(1)}, f32[4,128]{1,0:T(4,128)}, u32[]{:S(2)}) copy-start(f32[4,128]{1,0:T(4,128)} %param.17) | copy-start | bytes 6148
Sparse Core Ops, SparseCore 0:
  12.2 106.2 all-gather.3
where the time goes:
time: 230 us; the launch traced here: 229 us
  blocking collectives  109 us (47%)
  waiting for transfers between devices  38.3 us (17%)
  other arithmetic  38.2 us (17%)
  matrix products  17.4 us (8%)
  between operations  14.9 us (6%)
  starting transfers between devices  5.18 us (2%)
  local copies, waits for them, and re-layouts  4.62 us (2%)
    unnamed x1, blocking collectives  64.5 us
    psum x1, blocking collectives, local(): square_total = lax.psum(squares, 'tp')  44.4 us
    ppermute x4, waiting for transfers between devices, from_behind(): lax.ppermute(value, axis, [(source, source + steps) for source in range(i...  38.2 us
    add x31, other arithmetic, join_states(): jnp.exp(later[0])[:, None, None] * earlier[1] + later[1]  32.9 us
    dot_general x4, matrix products, dense_head(): jnp.einsum('te,se->ts', queries, key_rows, preferred_element_type=jnp.flo...  6.09 us
    ppermute x4, starting transfers between devices, from_behind(): lax.ppermute(value, axis, [(source, source + steps) for source in range(i...  5.15 us
  transfers between devices with their start and end apart: 5, of which 3 were waited for; matrix products, arithmetic and copies ran while one was open for 1% of the time, Pallas kernels for 0%

commit v1 on v0

v1 whole, which is shorter than its diff:
```python
import functools

import jax
import jax.numpy as jnp
from jax import lax
from jax.experimental import pallas as pl
from jax.experimental.pallas import tpu as pltpu
from jax.sharding import PartitionSpec as P

MESH = pl.DeviceIdType.MESH
F32, BF16 = jnp.float32, jnp.bfloat16
NX = 4
SPAN = 4
EPS = 1e-06
FAR = -1e30
HIGH = lax.Precision.HIGHEST


def ring(step, count):
    return min(step, count - step)


def mm(a, b, dims, precision=None):
    return lax.dot_general(a, b, (dims, ((), ())), precision=precision, preferred_element_type=F32)


def silu(v):
    v = v.astype(F32)
    return (v / (1.0 + jnp.exp(-v))).astype(BF16)


def kernel(
    nctx, ntp,
    ql_h, kl_h, vl_h, dec_ref, gain_ref, qs_h, ks_h, vs_h, doc_ref,
    light_h, att_h,
    ql, kl, vl, qs, kv, kact, sq, lin, light, att, bias,
    ub, p1, sb, p2, gb, g1, psb, ps1,
    lsem, u_s, u_r, g_s, g_r, c_s, c_r, p_s, p_r,
    s4_s, s4_r, s1_s, s1_r, s3_s, s3_r, sp_s, sp_r, sm_s, sm_r, osem,
):
    heads, rows, width = ql.shape
    ny, nz = nctx // NX, ntp // 2
    c, t = lax.axis_index("ctx"), lax.axis_index("tp")
    y, x = c // NX, lax.rem(c, NX)
    per = heads * width // nctx
    per_head = width // per

    around = [(dx, dy) for dx in range(NX) for dy in range(ny) if dx or dy]
    around.sort(key=lambda o: -(ring(o[0], NX) + ring(o[1], ny)))
    stack = [(dz, dc) for dz in range(nz) for dc in range(2) if dz or dc]
    stack.sort(key=lambda o: -(2 * ring(o[0], nz) + o[1]))

    def ctx_at(dx, dy):
        return lax.rem(y + dy, ny) * NX + lax.rem(x + dx, NX)

    def tp_at(dz, dc):
        return lax.rem(t // 2 + dz, nz) * 2 + lax.rem(lax.rem(t, 2) + dc, 2)

    barrier = pltpu.get_barrier_semaphore()
    for o in around:
        pl.semaphore_signal(barrier, inc=1, device_id=(ctx_at(*o), t), device_id_type=MESH)
    for o in stack:
        pl.semaphore_signal(barrier, inc=1, device_id=(c, tp_at(*o)), device_id_type=MESH)

    loads = [
        pltpu.make_async_copy(src, dst, lsem.at[i])
        for i, (src, dst) in enumerate(
            [(kl_h, kl), (vl_h, vl), (ks_h, kv.at[0, :, 0]), (vs_h, kv.at[0, :, 1]), (ql_h, ql), (qs_h, qs)]
        )
    ]
    for load in loads:
        load.start()

    early = lax.broadcasted_iota(jnp.int32, (rows, rows), 0)
    late = lax.broadcasted_iota(jnp.int32, (rows, rows), 1)
    cum = mm(dec_ref[...], (early <= late).astype(F32), ((1,), (0,)), HIGH)
    lane_head = lax.broadcasted_iota(jnp.int32, (heads, heads * width), 1) // width
    own_head = lax.broadcasted_iota(jnp.int32, (heads, heads * width), 0)
    spread = mm(cum, (lane_head == own_head).astype(F32), ((0,), (0,)), HIGH)

    def cols(h):
        return spread[:, h * width:(h + 1) * width]

    loads[0].wait()
    loads[1].wait()
    for h in range(heads):
        ch = cols(h)
        last = ch[rows - 1:rows, :]
        gb[h] = jnp.exp(last)
        k = silu(kl[h])
        kact[h] = k
        dk = (k.astype(F32) * jnp.exp(last - ch)).astype(BF16)
        u = mm(dk, vl[h], ((0,), (0,)))
        ub[pl.ds(h * per_head, per_head)] = u.astype(BF16).reshape(per_head, per, width)
    p1[c] = ub[c]
    g1[c] = gb[c // per_head]

    pl.semaphore_wait(barrier, len(around) + len(stack))

    def g_copy(o):
        p = ctx_at(*o)
        return pltpu.make_async_remote_copy(
            src_ref=gb.at[p // per_head], dst_ref=g1.at[c], send_sem=g_s, recv_sem=g_r,
            device_id=(p, t), device_id_type=MESH)

    def u_copy(o):
        p = ctx_at(*o)
        return pltpu.make_async_remote_copy(
            src_ref=ub.at[p], dst_ref=p1.at[c], send_sem=u_s, recv_sem=u_r,
            device_id=(p, t), device_id_type=MESH)

    def c_copy(o):
        p = ctx_at(*o)
        return pltpu.make_async_remote_copy(
            src_ref=sb.at[p], dst_ref=p2.at[c], send_sem=c_s, recv_sem=c_r,
            device_id=(p, t), device_id_type=MESH)

    def p_copy(o):
        return pltpu.make_async_remote_copy(
            src_ref=psb, dst_ref=ps1.at[t], send_sem=p_s, recv_sem=p_r,
            device_id=(c, tp_at(*o)), device_id_type=MESH)

    def wait_bytes(ref, count, sem):
        part = ref.at[pl.ds(0, count)]
        pltpu.make_async_copy(part, part, sem).wait()

    def move(src, dst, h, send, recv, to):
        return pltpu.make_async_remote_copy(
            src_ref=src, dst_ref=dst, send_sem=send.at[h], recv_sem=recv.at[h],
            device_id=(to, t), device_id_type=MESH)

    def s4(h):
        return move(kv.at[0, h], kv.at[4, h], h, s4_s, s4_r, ctx_at(0, 1))

    def s1(h):
        return move(kv.at[4 * (x // (NX - 1)), h], kv.at[1, h], h, s1_s, s1_r, ctx_at(1, 0))

    def s3(h):
        return move(kv.at[4 * ((x + NX - 1) // NX), h], kv.at[3, h], h, s3_s, s3_r, ctx_at(NX - 1, 0))

    def sp(h):
        return move(kv.at[1, h, 0], kv.at[2, h, 0], h, sp_s, sp_r, lax.rem(c + 1, nctx))

    def sm(h):
        return move(kv.at[3, h, 1], kv.at[2, h, 1], h, sm_s, sm_r, lax.rem(c + nctx - 1, nctx))

    def send_own(h):
        s4(h).start()

        @pl.when(x < NX - 1)
        def _():
            s1(h).start()

        @pl.when(x == 0)
        def _():
            s3(h).start()

    def pass_on(h):
        s4(h).wait_recv()

        @pl.when(x == NX - 1)
        def _():
            s1(h).start()

        @pl.when(x > 0)
        def _():
            s3(h).start()

    def pass_second(h):
        s1(h).wait_recv()
        sp(h).start()
        s3(h).wait_recv()
        sm(h).start()

    for o in around:
        g_copy(o).start()
    for o in around:
        u_copy(o).start()
    loads[2].wait()
    loads[3].wait()
    send_own(0)

    loads[4].wait()
    for h in range(heads):
        ch = cols(h)
        q = silu(ql[h])
        sq[h] = (q.astype(F32) * jnp.exp(ch)).astype(BF16)
        gap = jnp.concatenate([ch] * (rows // width), axis=1) - cum[h:h + 1, :]
        factor = jnp.where(early >= late, jnp.exp(jnp.minimum(gap, 0.0)), 0.0)
        w = (mm(q, kact[h], ((1,), (1,))) * factor).astype(BF16)
        lin[h] = mm(w, vl[h], ((1,), (0,)))

    wait_bytes(g1, nctx - 1, g_r)
    wait_bytes(p1, nctx - 1, u_r)
    state = jnp.zeros((per, width), F32)
    for d in range(nctx):
        sb[d] = state.astype(BF16)
        if d < nctx - 1:
            state = state * g1[d] + p1[d].astype(F32)
    p2[c] = sb[c]
    for o in around:
        c_copy(o).start()
    for h in range(1, heads):
        send_own(h)
    pass_on(0)

    where_q = c * rows + lax.broadcasted_iota(jnp.int32, (rows, width), 0)
    first = jnp.zeros((rows, width), jnp.int32)
    at = jnp.int32(0)
    for d in range(doc_ref.shape[0]):
        first = jnp.where(where_q >= at, jnp.maximum(first, at), first)
        at = at + doc_ref[d]
    first = jnp.concatenate([first] * (rows // width), axis=1)
    for k in range(SPAN + 1):
        keep = (c - k) * rows + late >= first
        if k == 0:
            keep = keep & (late <= early)
        bias[k] = jnp.where(keep, 0.0, FAR)

    wait_bytes(p2, nctx - 1, c_r)
    total = jnp.zeros((rows, width), F32)
    for h in range(heads):
        carried = p2[pl.ds(h * per_head, per_head)].reshape(width, width)
        out = lin[h] + mm(sq[h], carried, ((1,), (0,)))
        lin[h] = out
        total = total + out * out
    summed = mm(jnp.ones((8, width), F32), total, ((1,), (1,)), HIGH)[0:1, :]
    psb[...] = summed
    ps1[t] = summed
    for o in stack:
        p_copy(o).start()
    for h in range(1, heads):
        pass_on(h)
    pass_second(0)

    wait_bytes(ps1, ntp - 1, p_r)
    mean = mm(ps1[:, 0, :], jnp.ones((ntp, width), F32), ((0,), (0,)), HIGH) * (1.0 / (heads * ntp * width))
    scale = lax.rsqrt(mean + EPS)
    loads[5].wait()
    for h in range(heads):
        low = (lin[h] * scale * gain_ref[h:h + 1, :]).astype(BF16)
        light[h] = low
        qs[h] = (qs[h].astype(F32) + low.astype(F32)).astype(BF16)
    out_light = pltpu.make_async_copy(light, light_h, osem.at[heads])
    out_light.start()

    factor = width ** -0.5 * 1.4426950408889634
    for h in range(heads):
        if h + 1 < heads:
            pass_second(h + 1)
        sp(h).wait_recv()
        sm(h).wait_recv()
        q = qs[h]
        parts = [mm(q, kv[k, h, 0], ((1,), (1,))) + bias[k] for k in range(SPAN + 1)]
        top = parts[0]
        for part in parts[1:]:
            top = jnp.maximum(top, part)
        top = jnp.max(top, axis=1, keepdims=True)
        amount = jnp.zeros((rows, rows), F32)
        mixed = jnp.zeros((rows, width), F32)
        for k, part in enumerate(parts):
            weights = jnp.exp2((part - top) * factor)
            amount = amount + weights
            mixed = mixed + mm(weights.astype(BF16), kv[k, h, 1], ((1,), (0,)))
        att[h] = (mixed / jnp.sum(amount, axis=1, keepdims=True)).astype(BF16)
        pltpu.make_async_copy(att.at[h], att_h.at[h], osem.at[h]).start()

    out_light.wait()
    for h in range(heads):
        pltpu.make_async_copy(att.at[h], att_h.at[h], osem.at[h]).wait()
        for copy in (s4, s1, s3, sp, sm):
            copy(h).wait_send()
    wait_bytes(g1, nctx - 1, g_s)
    wait_bytes(p1, nctx - 1, u_s)
    wait_bytes(p2, nctx - 1, c_s)
    wait_bytes(ps1, ntp - 1, p_s)


def solution(mesh):
    nctx, ntp = mesh.shape["ctx"], mesh.shape["tp"]

    def local(ql, kl, vl, dec, gain, qs, ks, vs, doc):
        heads, rows, width = ql.shape
        per = heads * width // nctx
        any_ = pl.BlockSpec(memory_space=pl.ANY)
        vmem = pl.BlockSpec(memory_space=pltpu.VMEM)
        block = (heads, rows, width)
        dma = pltpu.SemaphoreType.DMA
        return tuple(pl.pallas_call(
            functools.partial(kernel, nctx, ntp),
            out_shape=[jax.ShapeDtypeStruct(block, BF16)] * 2,
            in_specs=[any_, any_, any_, vmem, vmem, any_, any_, any_, pl.BlockSpec(memory_space=pltpu.SMEM)],
            out_specs=[any_, any_],
            scratch_shapes=[
                pltpu.VMEM(block, BF16), pltpu.VMEM(block, BF16), pltpu.VMEM(block, BF16), pltpu.VMEM(block, BF16),
                pltpu.VMEM((SPAN + 1, heads, 2, rows, width), BF16),
                pltpu.VMEM(block, BF16), pltpu.VMEM(block, BF16), pltpu.VMEM(block, F32),
                pltpu.VMEM(block, BF16), pltpu.VMEM(block, BF16),
                pltpu.VMEM((SPAN + 1, rows, rows), F32),
                pltpu.VMEM((nctx, per, width), BF16), pltpu.VMEM((nctx, per, width), BF16),
                pltpu.VMEM((nctx, per, width), BF16), pltpu.VMEM((nctx, per, width), BF16),
                pltpu.VMEM((heads, 1, width), F32), pltpu.VMEM((nctx, 1, width), F32),
                pltpu.VMEM((1, rows), F32), pltpu.VMEM((ntp, 1, rows), F32),
                dma((6,)), dma, dma, dma, dma, dma, dma, dma, dma,
            ] + [dma((heads,))] * 10 + [dma((heads + 1,))],
            compiler_params=pltpu.CompilerParams(
                collective_id=0, has_side_effects=True, vmem_limit_bytes=60 << 20),
            cost_estimate=pl.CostEstimate(flops=900_000_000, bytes_accessed=4 << 20, transcendentals=2_000_000),
        )(ql, kl, vl, dec, gain, qs, ks, vs, doc))

    wide = P("tp", "ctx", None)
    return jax.shard_map(
        local, mesh=mesh,
        in_specs=(wide, wide, wide, P("tp", "ctx"), P("tp", None), wide, wide, wide, P()),
        out_specs=(wide, wide), check_vma=False)
```

time: 230 us -> 51.6 us (0.22)
  the two profiles are of different devices: /device:TPU:63 before, /device:TPU:6 now
where the time goes in v1:
time: 51.6 us; the launch traced here: 50.7 us
  Pallas kernels  47.6 us (92%)
  local copies, waits for them, and re-layouts  2.42 us (5%)
  between operations  0.65 us (1%)
    pallas_call x1, Pallas kernels, local(): pl.pallas_call(functools.partial(kernel, nctx, ntp), out_shape=[jax.Shape...  47.6 us
    unnamed x4, local copies, waits for them, and re-layouts  2.42 us

profile of v1, /device:TPU:6, one launch (start us, length us, event | category | flops | bytes accessed | tf_op | source)
XLA Modules:
  0.0 50.7 jit_solution(10356596649278178425)
XLA Ops:
  0.6 47.6 %shard_map.104 = (bf16[4,256,128]{2,1,0:T(8,128)(2,1)}, bf16[4,256,128]{2,1,0:T(8,128)(2,1)}) custom-call(bf16[4,256,128]{2,1,0:T(8,128)(2,1)} %ql_h.1, bf16[4,256,128]{2,1,0:T(8,128)(2,1)} %kl_h.1, bf16[4,256,128]{2,1,0:T(8,128)(2,1)} %vl_h.1, f32[4,256]{1,0:T(4,128)} %dec_ref.1, f32[4,128]{1,0:T(4,128)} %gain_ref.1, bf16[4,256,128]{2,1,0:T(8,128)(2,1)} %qs_h.1, ...), custom_call_target="tpu_custom_call" | custom-call | flops 900000000 | bytes 4194304 | tf_op jit(solution)/shard_map/pallas_call | solution.py:289
  48.3 0.0 copy-start
  48.3 1.7 %copy.13 = bf16[4,256,128]{2,1,0:T(8,128)(2,1)} copy(bf16[4,256,128]{2,1,0:T(8,128)(2,1)} %get-tuple-element.4) | data formatting | bytes 524288
  50.0 0.0 copy-done
  50.0 0.7 %copy.14 = bf16[4,256,128]{2,1,0:T(8,128)(2,1)} copy(bf16[4,256,128]{2,1,0:T(8,128)(2,1)S(1)} %copy-done) | data formatting | bytes 524288
Async XLA Ops:
  48.3 1.7 %copy-start = (bf16[4,256,128]{2,1,0:T(8,128)(2,1)S(1)}, bf16[4,256,128]{2,1,0:T(8,128)(2,1)}, u32[]{:S(2)}) copy-start(bf16[4,256,128]{2,1,0:T(8,128)(2,1)} %get-tuple-element.5) | copy-start | bytes 786436

commit v2 on v1

--- a/solution.py
+++ b/solution.py
@@ -13,6 +13,8 @@
 SPAN = 4
 EPS = 1e-06
 FAR = -1e30
+DIRECT = ()
+RIGHT = (0, 2, 4, 6)
 HIGH = lax.Precision.HIGHEST
 
 
@@ -36,7 +38,7 @@
     ql, kl, vl, qs, kv, kact, sq, lin, light, att, bias,
     ub, p1, sb, p2, gb, g1, psb, ps1,
     lsem, u_s, u_r, g_s, g_r, c_s, c_r, p_s, p_r,
-    s4_s, s4_r, s1_s, s1_r, s3_s, s3_r, sp_s, sp_r, sm_s, sm_r, osem,
+    s4_s, s4_r, s1_s, s1_r, s3_s, s3_r, s2_s, s2_r, osem, in_tp,
 ):
     heads, rows, width = ql.shape
     ny, nz = nctx // NX, ntp // 2
@@ -60,7 +62,9 @@
     for o in around:
         pl.semaphore_signal(barrier, inc=1, device_id=(ctx_at(*o), t), device_id_type=MESH)
     for o in stack:
-        pl.semaphore_signal(barrier, inc=1, device_id=(c, tp_at(*o)), device_id_type=MESH)
+        @pl.when(tp_at(*o) > t)
+        def _():
+            pl.semaphore_signal(barrier, inc=1, device_id=(c, tp_at(*o)), device_id_type=MESH)
 
     loads = [
         pltpu.make_async_copy(src, dst, lsem.at[i])
@@ -95,7 +99,11 @@
     p1[c] = ub[c]
     g1[c] = gb[c // per_head]
 
-    pl.semaphore_wait(barrier, len(around) + len(stack))
+    pl.semaphore_wait(barrier, len(around) + t)
+    for o in stack:
+        @pl.when(tp_at(*o) < t)
+        def _():
+            pl.semaphore_signal(in_tp, inc=1, device_id=(c, tp_at(*o)), device_id_type=MESH)
 
     def g_copy(o):
         p = ctx_at(*o)
@@ -124,53 +132,70 @@
         part = ref.at[pl.ds(0, count)]
         pltpu.make_async_copy(part, part, sem).wait()
 
-    def move(src, dst, h, send, recv, to):
-        return pltpu.make_async_remote_copy(
-            src_ref=src, dst_ref=dst, send_sem=send.at[h], recv_sem=recv.at[h],
-            device_id=(to, t), device_id_type=MESH)
-
-    def s4(h):
-        return move(kv.at[0, h], kv.at[4, h], h, s4_s, s4_r, ctx_at(0, 1))
-
-    def s1(h):
-        return move(kv.at[4 * (x // (NX - 1)), h], kv.at[1, h], h, s1_s, s1_r, ctx_at(1, 0))
-
-    def s3(h):
-        return move(kv.at[4 * ((x + NX - 1) // NX), h], kv.at[3, h], h, s3_s, s3_r, ctx_at(NX - 1, 0))
-
-    def sp(h):
-        return move(kv.at[1, h, 0], kv.at[2, h, 0], h, sp_s, sp_r, lax.rem(c + 1, nctx))
-
-    def sm(h):
-        return move(kv.at[3, h, 1], kv.at[2, h, 1], h, sm_s, sm_r, lax.rem(c + nctx - 1, nctx))
-
-    def send_own(h):
-        s4(h).start()
-
-        @pl.when(x < NX - 1)
-        def _():
-            s1(h).start()
-
-        @pl.when(x == 0)
-        def _():
-            s3(h).start()
-
-    def pass_on(h):
-        s4(h).wait_recv()
-
-        @pl.when(x == NX - 1)
-        def _():
-            s1(h).start()
-
-        @pl.when(x > 0)
-        def _():
-            s3(h).start()
-
-    def pass_second(h):
-        s1(h).wait_recv()
-        sp(h).start()
-        s3(h).wait_recv()
-        sm(h).start()
+    def move(q, src, dst, send, recv, to):
+        return pltpu.make_async_remote_copy(
+            src_ref=kv.at[src, q // 2, q % 2], dst_ref=kv.at[dst, q // 2, q % 2],
+            send_sem=send.at[q], recv_sem=recv.at[q], device_id=(to, t), device_id_type=MESH)
+
+    def s4(q):
+        return move(q, 0, 4, s4_s, s4_r, ctx_at(0, 1))
+
+    def s1(q):
+        return move(q, 4 * (x // (NX - 1)), 1, s1_s, s1_r, ctx_at(1, 0))
+
+    def s3(q):
+        return move(q, 4 * ((x + NX - 1) // NX), 3, s3_s, s3_r, ctx_at(NX - 1, 0))
+
+    def s3d(q):
+        return move(q, 0, 3, s3_s, s3_r, lax.rem(c + NX - 1, nctx))
+
+    def s2(q):
+        if q in RIGHT:
+            return move(q, 1, 2, s2_s, s2_r, lax.rem(c + 1, nctx))
+        return move(q, 3, 2, s2_s, s2_r, lax.rem(c + nctx - 1, nctx))
+
+    def down(*qs):
+        for q in qs:
+            s4(q).start()
+
+    def diag(*qs):
+        for q in qs:
+            @pl.when(x > 0)
+            def _():
+                s3d(q).start()
+
+    def own(*qs):
+        for q in qs:
+            @pl.when(x < NX - 1)
+            def _():
+                s1(q).start()
+
+            @pl.when(x == 0)
+            def _():
+                s3(q).start()
+
+    def on(*qs):
+        for q in qs:
+            s4(q).wait_recv()
+
+            @pl.when(x == NX - 1)
+            def _():
+                s1(q).start()
+
+            if q not in DIRECT:
+                @pl.when(x > 0)
+                def _():
+                    s3(q).start()
+
+    def second(*qs):
+        for q in qs:
+            (s1 if q in RIGHT else s3)(q).wait_recv()
+            s2(q).start()
+
+    def arrived(h):
+        for q in (2 * h, 2 * h + 1):
+            (s3 if q in RIGHT else s1)(q).wait_recv()
+            s2(q).wait_recv()
 
     for o in around:
         g_copy(o).start()
@@ -178,7 +203,8 @@
         u_copy(o).start()
     loads[2].wait()
     loads[3].wait()
-    send_own(0)
+    down(0,1,2,3)
+    own(0, 1, 2, 3)
 
     loads[4].wait()
     for h in range(heads):
@@ -200,9 +226,10 @@
     p2[c] = sb[c]
     for o in around:
         c_copy(o).start()
-    for h in range(1, heads):
-        send_own(h)
-    pass_on(0)
+    down(4, 5, 6, 7)
+    own(4, 5, 6, 7)
+    on(0,1,2)
+    second(0, 1)
 
     where_q = c * rows + lax.broadcasted_iota(jnp.int32, (rows, width), 0)
     first = jnp.zeros((rows, width), jnp.int32)
@@ -217,6 +244,8 @@
             keep = keep & (late <= early)
         bias[k] = jnp.where(keep, 0.0, FAR)
 
+    on(3)
+    second(2)
     wait_bytes(p2, nctx - 1, c_r)
     total = jnp.zeros((rows, width), F32)
     for h in range(heads):
@@ -227,11 +256,20 @@
     summed = mm(jnp.ones((8, width), F32), total, ((1,), (1,)), HIGH)[0:1, :]
     psb[...] = summed
     ps1[t] = summed
+    @pl.when(t < ntp - 1)
+    def _():
+        pl.semaphore_wait(in_tp, ntp - 1 - t)
+
     for o in stack:
         p_copy(o).start()
-    for h in range(1, heads):
-        pass_on(h)
-    pass_second(0)
+    on(4)
+    second(3)
+    on(5)
+    second(4)
+    on(6)
+    second(5)
+    on(7)
+    second(6, 7)
 
     wait_bytes(ps1, ntp - 1, p_r)
     mean = mm(ps1[:, 0, :], jnp.ones((ntp, width), F32), ((0,), (0,)), HIGH) * (1.0 / (heads * ntp * width))
@@ -246,10 +284,7 @@
 
     factor = width ** -0.5 * 1.4426950408889634
     for h in range(heads):
-        if h + 1 < heads:
-            pass_second(h + 1)
-        sp(h).wait_recv()
-        sm(h).wait_recv()
+        arrived(h)
         q = qs[h]
         parts = [mm(q, kv[k, h, 0], ((1,), (1,))) + bias[k] for k in range(SPAN + 1)]
         top = parts[0]
@@ -268,8 +303,9 @@
     out_light.wait()
     for h in range(heads):
         pltpu.make_async_copy(att.at[h], att_h.at[h], osem.at[h]).wait()
-        for copy in (s4, s1, s3, sp, sm):
-            copy(h).wait_send()
+        for q in (2 * h, 2 * h + 1):
+            for copy in (s4, s1, s3, s2):
+                copy(q).wait_send()
     wait_bytes(g1, nctx - 1, g_s)
     wait_bytes(p1, nctx - 1, u_s)
     wait_bytes(p2, nctx - 1, c_s)
@@ -302,7 +338,7 @@
                 pltpu.VMEM((heads, 1, width), F32), pltpu.VMEM((nctx, 1, width), F32),
                 pltpu.VMEM((1, rows), F32), pltpu.VMEM((ntp, 1, rows), F32),
                 dma((6,)), dma, dma, dma, dma, dma, dma, dma, dma,
-            ] + [dma((heads,))] * 10 + [dma((heads + 1,))],
+            ] + [dma((2 * heads,))] * 8 + [dma((heads + 1,)), pltpu.SemaphoreType.REGULAR],
             compiler_params=pltpu.CompilerParams(
                 collective_id=0, has_side_effects=True, vmem_limit_bytes=60 << 20),
             cost_estimate=pl.CostEstimate(flops=900_000_000, bytes_accessed=4 << 20, transcendentals=2_000_000),

time: 51.6 us -> 46 us (0.89); the launches traced: 50.7 us -> 45.8 us
  Pallas kernels: 47.6 us -> 42.7 us
    pallas_call x1, Pallas kernels: 47.6 us -> 42.7 us  [local(): pl.pallas_call(functools.partial(kernel, nctx, ntp), out_shape=[jax.Shape...]
where the time goes in v2:
time: 46 us; the launch traced here: 45.8 us
  Pallas kernels  42.7 us (93%)
  local copies, waits for them, and re-layouts  2.42 us (5%)
  between operations  0.65 us (1%)
    pallas_call x1, Pallas kernels, local(): pl.pallas_call(functools.partial(kernel, nctx, ntp), out_shape=[jax.Shape...  42.7 us
    unnamed x4, local copies, waits for them, and re-layouts  2.42 us

profile of v2, /device:TPU:6, one launch (start us, length us, event | category | flops | bytes accessed | tf_op | source)
XLA Modules:
  0.0 45.8 jit_solution(10844017418395014446)
XLA Ops:
  0.6 42.7 %shard_map.104 = (bf16[4,256,128]{2,1,0:T(8,128)(2,1)}, bf16[4,256,128]{2,1,0:T(8,128)(2,1)}) custom-call(bf16[4,256,128]{2,1,0:T(8,128)(2,1)} %ql_h.1, bf16[4,256,128]{2,1,0:T(8,128)(2,1)} %kl_h.1, bf16[4,256,128]{2,1,0:T(8,128)(2,1)} %vl_h.1, f32[4,256]{1,0:T(4,128)} %dec_ref.1, f32[4,128]{1,0:T(4,128)} %gain_ref.1, bf16[4,256,128]{2,1,0:T(8,128)(2,1)} %qs_h.1, ...), custom_call_target="tpu_custom_call" | custom-call | flops 900000000 | bytes 4194304 | tf_op jit(solution)/shard_map/pallas_call | solution.py:325
  43.4 0.0 copy-start
  43.4 1.7 %copy.13 = bf16[4,256,128]{2,1,0:T(8,128)(2,1)} copy(bf16[4,256,128]{2,1,0:T(8,128)(2,1)} %get-tuple-element.4) | data formatting | bytes 524288
  45.1 0.0 copy-done
  45.1 0.7 %copy.14 = bf16[4,256,128]{2,1,0:T(8,128)(2,1)} copy(bf16[4,256,128]{2,1,0:T(8,128)(2,1)S(1)} %copy-done) | data formatting | bytes 524288
Async XLA Ops:
  43.4 1.7 %copy-start = (bf16[4,256,128]{2,1,0:T(8,128)(2,1)S(1)}, bf16[4,256,128]{2,1,0:T(8,128)(2,1)}, u32[]{:S(2)}) copy-start(bf16[4,256,128]{2,1,0:T(8,128)(2,1)} %get-tuple-element.5) | copy-start | bytes 786436

commit v3 on v2

--- a/solution.py
+++ b/solution.py
@@ -34,7 +34,7 @@
 def kernel(
     nctx, ntp,
     ql_h, kl_h, vl_h, dec_ref, gain_ref, qs_h, ks_h, vs_h, doc_ref,
-    light_h, att_h,
+    out_h,
     ql, kl, vl, qs, kv, kact, sq, lin, light, att, bias,
     ub, p1, sb, p2, gb, g1, psb, ps1,
     lsem, u_s, u_r, g_s, g_r, c_s, c_r, p_s, p_r,
@@ -279,7 +279,7 @@
         low = (lin[h] * scale * gain_ref[h:h + 1, :]).astype(BF16)
         light[h] = low
         qs[h] = (qs[h].astype(F32) + low.astype(F32)).astype(BF16)
-    out_light = pltpu.make_async_copy(light, light_h, osem.at[heads])
+    out_light = pltpu.make_async_copy(light, out_h.at[0], osem.at[heads])
     out_light.start()
 
     factor = width ** -0.5 * 1.4426950408889634
@@ -298,11 +298,11 @@
             amount = amount + weights
             mixed = mixed + mm(weights.astype(BF16), kv[k, h, 1], ((1,), (0,)))
         att[h] = (mixed / jnp.sum(amount, axis=1, keepdims=True)).astype(BF16)
-        pltpu.make_async_copy(att.at[h], att_h.at[h], osem.at[h]).start()
+        pltpu.make_async_copy(att.at[h], out_h.at[1, h], osem.at[h]).start()
 
     out_light.wait()
     for h in range(heads):
-        pltpu.make_async_copy(att.at[h], att_h.at[h], osem.at[h]).wait()
+        pltpu.make_async_copy(att.at[h], out_h.at[1, h], osem.at[h]).wait()
         for q in (2 * h, 2 * h + 1):
             for copy in (s4, s1, s3, s2):
                 copy(q).wait_send()
@@ -322,11 +322,11 @@
         vmem = pl.BlockSpec(memory_space=pltpu.VMEM)
         block = (heads, rows, width)
         dma = pltpu.SemaphoreType.DMA
-        return tuple(pl.pallas_call(
+        both = pl.pallas_call(
             functools.partial(kernel, nctx, ntp),
-            out_shape=[jax.ShapeDtypeStruct(block, BF16)] * 2,
+            out_shape=jax.ShapeDtypeStruct((2,) + block, BF16),
             in_specs=[any_, any_, any_, vmem, vmem, any_, any_, any_, pl.BlockSpec(memory_space=pltpu.SMEM)],
-            out_specs=[any_, any_],
+            out_specs=any_,
             scratch_shapes=[
                 pltpu.VMEM(block, BF16), pltpu.VMEM(block, BF16), pltpu.VMEM(block, BF16), pltpu.VMEM(block, BF16),
                 pltpu.VMEM((SPAN + 1, heads, 2, rows, width), BF16),
@@ -342,7 +342,8 @@
             compiler_params=pltpu.CompilerParams(
                 collective_id=0, has_side_effects=True, vmem_limit_bytes=60 << 20),
             cost_estimate=pl.CostEstimate(flops=900_000_000, bytes_accessed=4 << 20, transcendentals=2_000_000),
-        )(ql, kl, vl, dec, gain, qs, ks, vs, doc))
+        )(ql, kl, vl, dec, gain, qs, ks, vs, doc)
+        return both[0], both[1]
 
     wide = P("tp", "ctx", None)
     return jax.shard_map(

time: 46 us -> 45.4 us (0.987)
  local copies, waits for them, and re-layouts: 2.42 us -> 1.86 us
    unnamed x4 -> x0, local copies, waits for them, and re-layouts: 2.42 us -> none
    squeeze x0 -> x1, local copies, waits for them, and re-layouts: none -> 1.86 us  [local(): return (both[0], both[1])]
where the time goes in v3:
time: 45.4 us; the launch traced here: 45.2 us
  Pallas kernels  42.7 us (94%)
  local copies, waits for them, and re-layouts  1.86 us (4%)
  between operations  0.64 us (1%)
    pallas_call x1, Pallas kernels, local(): pl.pallas_call(functools.partial(kernel, nctx, ntp), out_shape=jax.ShapeD...  42.7 us
    squeeze x1, local copies, waits for them, and re-layouts, local(): return (both[0], both[1])  1.86 us

profile of v3, /device:TPU:6, one launch (start us, length us, event | category | flops | bytes accessed | tf_op | source)
XLA Modules:
  0.0 45.2 jit_solution(14153949091894225639)
XLA Ops:
  0.6 42.7 %shard_map.104 = bf16[2,4,256,128]{3,2,1,0:T(8,128)(2,1)} custom-call(bf16[4,256,128]{2,1,0:T(8,128)(2,1)} %ql_h.1, bf16[4,256,128]{2,1,0:T(8,128)(2,1)} %kl_h.1, bf16[4,256,128]{2,1,0:T(8,128)(2,1)} %vl_h.1, f32[4,256]{1,0:T(4,128)} %dec_ref.1, f32[4,128]{1,0:T(4,128)} %gain_ref.1, bf16[4,256,128]{2,1,0:T(8,128)(2,1)} %qs_h.1, bf16[4,256,128]{2,1,0:T(8,128)(2,1)} %ks_h.1, ...), custom_call_target="tpu_custom_call" | custom-call | flops 900000000 | bytes 4194304 | tf_op jit(solution)/shard_map/pallas_call | solution.py:325
  43.4 1.9 %slice_bitcast_fusion = (bf16[4,256,128]{2,1,0:T(8,128)(2,1)}, bf16[4,256,128]{2,1,0:T(8,128)(2,1)}) fusion(bf16[2,4,256,128]{3,2,1,0:T(8,128)(2,1)} %shard_map.104), kind=kLoop, calls=%fused_computation | loop fusion | bytes 1048576 | tf_op jit(solution)/shard_map/squeeze | solution.py:346

commit v4 on v3

--- a/solution.py
+++ b/solution.py
@@ -14,7 +14,7 @@
 EPS = 1e-06
 FAR = -1e30
 DIRECT = ()
-RIGHT = (0, 2, 4, 6)
+RIGHT = (2, 4, 6, 7)
 HIGH = lax.Precision.HIGHEST
 
 
@@ -216,6 +216,7 @@
         w = (mm(q, kact[h], ((1,), (1,))) * factor).astype(BF16)
         lin[h] = mm(w, vl[h], ((1,), (0,)))
 
+    on(0)
     wait_bytes(g1, nctx - 1, g_r)
     wait_bytes(p1, nctx - 1, u_r)
     state = jnp.zeros((per, width), F32)
@@ -228,8 +229,10 @@
         c_copy(o).start()
     down(4, 5, 6, 7)
     own(4, 5, 6, 7)
-    on(0,1,2)
-    second(0, 1)
+    on(1)
+    second(0)
+    on(2)
+    second(1)
 
     where_q = c * rows + lax.broadcasted_iota(jnp.int32, (rows, width), 0)
     first = jnp.zeros((rows, width), jnp.int32)

time: 45.4 us -> 45.6 us (level)
  the two profiles are of different devices: /device:TPU:6 before, /device:TPU:448 now
where the time goes in v4:
time: 45.6 us; the launch traced here: 45.5 us
  Pallas kernels  43 us (94%)
  local copies, waits for them, and re-layouts  1.86 us (4%)
  between operations  0.64 us (1%)
    pallas_call x1, Pallas kernels, local(): pl.pallas_call(functools.partial(kernel, nctx, ntp), out_shape=jax.ShapeD...  43 us
    squeeze x1, local copies, waits for them, and re-layouts, local(): return (both[0], both[1])  1.86 us

profile of v4, /device:TPU:448, one launch (start us, length us, event | category | flops | bytes accessed | tf_op | source)
XLA Modules:
  0.0 45.5 jit_solution(4368272056862485050)
XLA Ops:
  0.6 43.0 %shard_map.104 = bf16[2,4,256,128]{3,2,1,0:T(8,128)(2,1)} custom-call(bf16[4,256,128]{2,1,0:T(8,128)(2,1)} %ql_h.1, bf16[4,256,128]{2,1,0:T(8,128)(2,1)} %kl_h.1, bf16[4,256,128]{2,1,0:T(8,128)(2,1)} %vl_h.1, f32[4,256]{1,0:T(4,128)} %dec_ref.1, f32[4,128]{1,0:T(4,128)} %gain_ref.1, bf16[4,256,128]{2,1,0:T(8,128)(2,1)} %qs_h.1, bf16[4,256,128]{2,1,0:T(8,128)(2,1)} %ks_h.1, ...), custom_call_target="tpu_custom_call" | custom-call | flops 900000000 | bytes 4194304 | tf_op jit(solution)/shard_map/pallas_call | solution.py:328
  43.6 1.9 %slice_bitcast_fusion = (bf16[4,256,128]{2,1,0:T(8,128)(2,1)}, bf16[4,256,128]{2,1,0:T(8,128)(2,1)}) fusion(bf16[2,4,256,128]{3,2,1,0:T(8,128)(2,1)} %shard_map.104), kind=kLoop, calls=%fused_computation | loop fusion | bytes 1048576 | tf_op jit(solution)/shard_map/squeeze | solution.py:349
